TPU v7x, 32 devices: a whole 2x2x4 slice. The times are simulated.
32 devices in a mesh: section: 2 (over core), fsdp: 4 (over y, x), replica: 4 (over z).
Axes of the slice: x: 2, y: 2, z: 4, core: 2. Of those that a mesh axis runs over, the one named last changes fastest.
Arguments:
- images: bfloat16 [64, 196, 512], P(('fsdp', 'replica')), may hold values from -6 to 6
- cotangent: bfloat16 [64, 196, 512], P(('fsdp', 'replica')), may hold values from -6 to 6
- ln1_gain: float32 [2, 512], P('section'), may hold values from 0.5 to 1.5
- ln1_bias: float32 [2, 512], P('section'), may hold values from -1.75 to 1.75
- qkv_weight: bfloat16 [2, 512, 1536], P('section', 'fsdp'), may hold values from -0.25 to 0.25
- qkv_bias: float32 [2, 1536], P('section'), may hold values from -1.75 to 1.75
- proj_weight: bfloat16 [2, 512, 512], P('section', 'fsdp'), may hold values from -1 to 1
- proj_bias: float32 [2, 512], P('section'), may hold values from -1.75 to 1.75
- ln2_gain: float32 [2, 512], P('section'), may hold values from 0.5 to 1.5
- ln2_bias: float32 [2, 512], P('section'), may hold values from -1.75 to 1.75
- fc1_weight: bfloat16 [2, 512, 2048], P('section', 'fsdp'), may hold values from -0.25 to 0.25
- fc1_bias: float32 [2, 2048], P('section'), may hold values from -1.75 to 1.75
- fc2_weight: bfloat16 [2, 2048, 512], P('section', 'fsdp'), may hold values from -0.1875 to 0.1875
- fc2_bias: float32 [2, 512], P('section'), may hold values from -1.75 to 1.75
- rel_table: float32 [2, 169, 16], P('section'), may hold values from -6 to 6
- rel_index: int32 [49, 49], replicated, may hold values from 0 to 168
- region: int32 [196], replicated, may hold values from 0 to 8, as said below
Outputs:
- activations: bfloat16 [2, 64, 196, 512], P('section', ('fsdp', 'replica'))
- input_grad: bfloat16 [2, 64, 196, 512], P('section', ('fsdp', 'replica'))
- grad_ln1_gain: float32 [2, 512], P('section')
- grad_ln1_bias: float32 [2, 512], P('section')
- grad_qkv_weight: float32 [2, 512, 1536], P('section', 'fsdp')
- grad_qkv_bias: float32 [2, 1536], P('section')
- grad_proj_weight: float32 [2, 512, 512], P('section', 'fsdp')
- grad_proj_bias: float32 [2, 512], P('section')
- grad_ln2_gain: float32 [2, 512], P('section')
- grad_ln2_bias: float32 [2, 512], P('section')
- grad_fc1_weight: float32 [2, 512, 2048], P('section', 'fsdp')
- grad_fc1_bias: float32 [2, 2048], P('section')
- grad_fc2_weight: float32 [2, 2048, 512], P('section', 'fsdp')
- grad_fc2_bias: float32 [2, 512], P('section')
- grad_rel_table: float32 [2, 169, 16], P('section')
Inputs may be any that keep to these rules, and one draw needn't show every extreme that they name: `region`: labels of axis-aligned blocks, three bands of rows times three bands of columns, each band a run of positions.
All inputs are finite; a program needn't handle non-finite values.
Results may differ from a plain program's by a relative error of at most 0.019.
Values may be sent and summed in bfloat16 or wider, within the bound.
A program may use at most 192 MiB of HBM per device.

v0:
```python
import jax
import jax.numpy as jnp
from jax import lax
from jax.sharding import PartitionSpec as P

D = 512
HEADS = 16
HEAD_DIM = 32
FF = 2048
WIN = 7
SHIFT = 3
SIDE = 14
REL = 169
MICRO = 2
IMG_MB = 2


def shifted(value, axis, steps):
    count = lax.axis_size(axis)
    initial, last = (max(0, -steps), min(count, count - steps))
    return lax.ppermute(value, axis, [(source, source + steps) for source in range(initial, last)])


def layer_norm(values, gain, offset):
    centre = values - jnp.mean(values, -1, keepdims=True)
    spread = jnp.mean(centre * centre, -1, keepdims=True)
    return centre * lax.rsqrt(spread + 1e-05) * gain + offset


def to_windows(field):
    count = field.shape[0]
    across = SIDE // WIN
    field = field.reshape(count, across, WIN, across, WIN, field.shape[-1])
    field = field.transpose(0, 1, 3, 2, 4, 5)
    return field.reshape(count * across * across, WIN * WIN, field.shape[-1])


def from_windows(blocks, count):
    across = SIDE // WIN
    blocks = blocks.reshape(count, across, across, WIN, WIN, blocks.shape[-1])
    blocks = blocks.transpose(0, 1, 3, 2, 4, 5)
    return blocks.reshape(count, SIDE, SIDE, blocks.shape[-1])


def roll_into(grid, first):
    return jnp.where(first, grid, jnp.roll(grid, (-SHIFT, -SHIFT), (1, 2)))


def roll_back(grid, first):
    return jnp.where(first, grid, jnp.roll(grid, (SHIFT, SHIFT), (1, 2)))


def split_heads(packed):
    return packed.reshape(-1, WIN * WIN, 3, HEADS, HEAD_DIM).transpose(2, 0, 3, 1, 4)


def row_product(left, right):
    return jnp.einsum(
        "ri,rj->ij",
        left.reshape(-1, left.shape[-1]),
        right.reshape(-1, right.shape[-1]),
        preferred_element_type=jnp.float32,
    )


def forward_layer(inputs, weights, small, first, table_bias, penalty):
    w_qkv, w_proj, w_fc1, w_fc2 = weights
    gain_one, shift_one, bias_qkv, bias_proj, gain_two, shift_two, bias_fc1, bias_fc2 = small
    count = inputs.shape[0]
    normed = layer_norm(inputs, gain_one, shift_one).astype(jnp.bfloat16)
    windows = to_windows(roll_into(normed.reshape(count, SIDE, SIDE, D), first))
    packed = (jnp.dot(windows, w_qkv, preferred_element_type=jnp.float32) + bias_qkv).astype(
        jnp.bfloat16
    )
    heads = split_heads(packed)
    scores = jnp.einsum(
        "bhid,bhjd->bhij", heads[0], heads[1], preferred_element_type=jnp.float32
    ) * HEAD_DIM ** (-0.5)
    scores = scores + table_bias
    scores = scores.reshape(count, -1, HEADS, WIN * WIN, WIN * WIN) + penalty[None, :, None]
    probs = jax.nn.softmax(scores, -1).reshape(-1, HEADS, WIN * WIN, WIN * WIN)
    mixed = jnp.einsum(
        "bhij,bhjd->bihd", probs.astype(jnp.bfloat16), heads[2], preferred_element_type=jnp.float32
    )
    attended = mixed.reshape(-1, WIN * WIN, D).astype(jnp.bfloat16)
    branch = jnp.dot(attended, w_proj, preferred_element_type=jnp.float32) + bias_proj
    branch = roll_back(from_windows(branch, count), first)
    middle = inputs + branch.reshape(count, SIDE * SIDE, D)
    normed_two = layer_norm(middle, gain_two, shift_two).astype(jnp.bfloat16)
    hidden = jnp.dot(normed_two, w_fc1, preferred_element_type=jnp.float32) + bias_fc1
    activated = jax.nn.gelu(hidden, approximate=False).astype(jnp.bfloat16)
    output = middle + (jnp.dot(activated, w_fc2, preferred_element_type=jnp.float32) + bias_fc2)
    return (output, (inputs, packed, probs, attended, middle, hidden))


def gelu_exact(values):
    return jax.nn.gelu(values, approximate=False)


def backward_layer(grad_out, kept, weights, small, first, onehot):
    inputs, packed, probs, attended, middle, hidden = kept
    w_qkv, w_proj, w_fc1, w_fc2 = weights
    gain_one, shift_one, bias_qkv, bias_proj, gain_two, shift_two, bias_fc1, bias_fc2 = small
    count = inputs.shape[0]
    grad_mlp = grad_out.astype(jnp.bfloat16)
    activated, gelu_pull = jax.vjp(gelu_exact, hidden)
    grad_fc2 = row_product(activated.astype(jnp.bfloat16), grad_mlp)
    grad_bias_fc2 = jnp.sum(grad_mlp.astype(jnp.float32), (0, 1))
    grad_act = jnp.dot(grad_mlp, w_fc2.T, preferred_element_type=jnp.float32)
    grad_hidden = gelu_pull(grad_act)[0].astype(jnp.bfloat16)
    normed_two, norm_two_pull = jax.vjp(layer_norm, middle, gain_two, shift_two)
    grad_fc1 = row_product(normed_two.astype(jnp.bfloat16), grad_hidden)
    grad_bias_fc1 = jnp.sum(grad_hidden.astype(jnp.float32), (0, 1))
    grad_normed_two = jnp.dot(grad_hidden, w_fc1.T, preferred_element_type=jnp.float32)
    grad_middle, grad_gain_two, grad_shift_two = norm_two_pull(grad_normed_two)
    grad_middle = grad_middle + grad_out
    grad_branch = to_windows(
        roll_into(grad_middle.reshape(count, SIDE, SIDE, D), first).astype(jnp.bfloat16)
    )
    grad_proj = row_product(attended, grad_branch)
    grad_bias_proj = jnp.sum(grad_branch.astype(jnp.float32), (0, 1))
    grad_att = jnp.dot(grad_branch, w_proj.T, preferred_element_type=jnp.float32).astype(
        jnp.bfloat16
    )
    grad_att = grad_att.reshape(-1, WIN * WIN, HEADS, HEAD_DIM)
    heads = split_heads(packed)
    grad_probs = jnp.einsum(
        "bihd,bhjd->bhij", grad_att, heads[2], preferred_element_type=jnp.float32
    )
    grad_values = jnp.einsum(
        "bhij,bihd->bjhd", probs.astype(jnp.bfloat16), grad_att, preferred_element_type=jnp.float32
    )
    grad_scores = probs * (grad_probs - jnp.sum(grad_probs * probs, -1, keepdims=True))
    scores_low = grad_scores.astype(jnp.bfloat16)
    grad_bias_heads = jnp.sum(scores_low.astype(jnp.float32), 0).reshape(HEADS, -1)
    grad_table = jnp.dot(onehot.T, grad_bias_heads.T, precision=lax.Precision.HIGHEST)
    grad_query = jnp.einsum(
        "bhij,bhjd->bihd", scores_low, heads[1], preferred_element_type=jnp.float32
    ) * HEAD_DIM ** (-0.5)
    grad_keys = jnp.einsum(
        "bhij,bhid->bjhd", scores_low, heads[0], preferred_element_type=jnp.float32
    ) * HEAD_DIM ** (-0.5)
    grad_packed = (
        jnp.stack([grad_query, grad_keys, grad_values], 2)
        .reshape(-1, WIN * WIN, 3 * D)
        .astype(jnp.bfloat16)
    )
    normed, norm_one_pull = jax.vjp(layer_norm, inputs, gain_one, shift_one)
    windows = to_windows(
        roll_into(normed.astype(jnp.bfloat16).reshape(count, SIDE, SIDE, D), first)
    )
    grad_qkv = row_product(windows, grad_packed)
    grad_bias_qkv = jnp.sum(grad_packed.astype(jnp.float32), (0, 1))
    grad_windows = jnp.dot(grad_packed, w_qkv.T, preferred_element_type=jnp.float32)
    grad_grid = roll_back(from_windows(grad_windows, count), first)
    grad_in, grad_gain_one, grad_shift_one = norm_one_pull(grad_grid.reshape(count, SIDE * SIDE, D))
    grad_in = grad_in + grad_middle
    large = (grad_qkv, grad_proj, grad_fc1, grad_fc2)
    minor = (
        grad_gain_one,
        grad_shift_one,
        grad_bias_qkv,
        grad_bias_proj,
        grad_gain_two,
        grad_shift_two,
        grad_bias_fc1,
        grad_bias_fc2,
        grad_table,
    )
    return (grad_in, large, minor)


def on_device(
    images,
    cotangent,
    ln1_gain,
    ln1_bias,
    qkv_weight,
    qkv_bias,
    proj_weight,
    proj_bias,
    ln2_gain,
    ln2_bias,
    fc1_weight,
    fc1_bias,
    fc2_weight,
    fc2_bias,
    rel_table,
    rel_index,
    region,
):
    section = lax.axis_index("section")
    first = section == 0
    small = tuple(
        (
            item[0]
            for item in (
                ln1_gain,
                ln1_bias,
                qkv_bias,
                proj_bias,
                ln2_gain,
                ln2_bias,
                fc1_bias,
                fc2_bias,
            )
        )
    )
    onehot = (rel_index.reshape(-1, 1) == jnp.arange(REL, dtype=jnp.int32)[None, :]).astype(
        jnp.float32
    )
    table_bias = jnp.dot(onehot, rel_table[0], precision=lax.Precision.HIGHEST).T.reshape(
        HEADS, WIN * WIN, WIN * WIN
    )
    labels = to_windows(region.reshape(1, SIDE, SIDE, 1))[:, :, 0]
    differs = labels[:, :, None] != labels[:, None, :]
    penalty = jnp.where(jnp.logical_and(differs, jnp.logical_not(first)), -100.0, 0.0).astype(
        jnp.float32
    )
    count = IMG_MB
    moments = MICRO + 1

    def fetch_forward():
        full = (
            lax.all_gather(qkv_weight, "fsdp", axis=1, tiled=True),
            lax.all_gather(proj_weight, "fsdp", axis=1, tiled=True),
            lax.all_gather(fc1_weight, "fsdp", axis=1, tiled=True),
            lax.all_gather(fc2_weight, "fsdp", axis=1, tiled=True),
        )
        return tuple((piece[0] for piece in full))

    def fetch_backward():
        full = (
            lax.all_gather(qkv_weight, "fsdp", axis=1, tiled=True),
            lax.all_gather(proj_weight, "fsdp", axis=1, tiled=True),
            lax.all_gather(fc1_weight, "fsdp", axis=1, tiled=True),
            lax.all_gather(fc2_weight, "fsdp", axis=1, tiled=True),
        )
        return tuple((piece[0] for piece in full))

    received = jnp.zeros((count, SIDE * SIDE, D), jnp.bfloat16)
    saved = []
    produced = []
    for moment in range(moments):
        if moment < MICRO:
            own = images[moment * count : (moment + 1) * count].astype(jnp.float32)
        else:
            own = jnp.zeros((count, SIDE * SIDE, D), jnp.float32)
        inputs = jnp.where(first, own, received.astype(jnp.float32))
        weights = fetch_forward()
        output, kept = forward_layer(inputs, weights, small, first, table_bias, penalty)
        saved.append(kept)
        sent = output.astype(jnp.bfloat16)
        produced.append(sent)
        if moment < moments - 1:
            received = shifted(sent, "section", 1)
    activations = jnp.where(
        first, jnp.concatenate(produced[:MICRO], 0), jnp.concatenate(produced[1:], 0)
    )
    large_total = (
        jnp.zeros((D, 3 * D), jnp.float32),
        jnp.zeros((D, D), jnp.float32),
        jnp.zeros((D, FF), jnp.float32),
        jnp.zeros((FF, D), jnp.float32),
    )
    owned_total = None
    minor_total = None
    back_in = jnp.zeros((count, SIDE * SIDE, D), jnp.bfloat16)
    returned = []
    for moment in range(moments):
        if moment < MICRO:
            own_grad = cotangent[moment * count : (moment + 1) * count].astype(jnp.float32)
        else:
            own_grad = jnp.zeros((count, SIDE * SIDE, D), jnp.float32)
        active = jnp.where(first, float(moment >= 1), float(moment < MICRO)).astype(jnp.float32)
        grad_out = jnp.where(first, back_in.astype(jnp.float32), own_grad) * active
        kept = jax.tree.map(
            lambda early, later: jnp.where(first, early, later),
            saved[max(moment - 1, 0)],
            saved[min(moment + 1, MICRO)],
        )
        weights = fetch_backward()
        grad_in, large, minor = backward_layer(grad_out, kept, weights, small, first, onehot)
        sent_grad = grad_in.astype(jnp.bfloat16)
        returned.append(sent_grad)
        large_total = tuple((left + right for left, right in zip(large_total, large)))
        minor_total = (
            minor
            if minor_total is None
            else tuple((left + right for left, right in zip(minor_total, minor)))
        )
        if moment < moments - 1:
            back_in = shifted(sent_grad, "section", -1)
    input_grad = jnp.where(
        first, jnp.concatenate(returned[1:], 0), jnp.concatenate(returned[:MICRO], 0)
    )
    owned_total = (
        lax.psum_scatter(
            large_total[0][None].astype(jnp.bfloat16), "fsdp", scatter_dimension=1, tiled=True
        ).astype(jnp.float32),
        lax.psum_scatter(
            large_total[1][None].astype(jnp.bfloat16), "fsdp", scatter_dimension=1, tiled=True
        ).astype(jnp.float32),
        lax.psum_scatter(
            large_total[2][None].astype(jnp.bfloat16), "fsdp", scatter_dimension=1, tiled=True
        ).astype(jnp.float32),
        lax.psum_scatter(
            large_total[3][None].astype(jnp.bfloat16), "fsdp", scatter_dimension=1, tiled=True
        ).astype(jnp.float32),
    )
    owned = (
        lax.psum(owned_total[0].astype(jnp.bfloat16), "replica").astype(jnp.float32),
        lax.psum(owned_total[1].astype(jnp.bfloat16), "replica").astype(jnp.float32),
        lax.psum(owned_total[2].astype(jnp.bfloat16), "replica").astype(jnp.float32),
        lax.psum(owned_total[3].astype(jnp.bfloat16), "replica").astype(jnp.float32),
    )
    minors = lax.psum(
        (
            minor_total[0],
            minor_total[1],
            minor_total[2],
            minor_total[3],
            minor_total[4],
            minor_total[5],
            minor_total[6],
            minor_total[7],
            minor_total[8],
        ),
        ("fsdp", "replica"),
    )
    return (
        activations[None],
        input_grad[None],
        minors[0][None],
        minors[1][None],
        owned[0],
        minors[2][None],
        owned[1],
        minors[3][None],
        minors[4][None],
        minors[5][None],
        owned[2],
        minors[6][None],
        owned[3],
        minors[7][None],
        minors[8][None],
    )


def solution(mesh):
    in_specs = (
        P(("fsdp", "replica"), None, None),
        P(("fsdp", "replica"), None, None),
        P("section", None),
        P("section", None),
        P("section", "fsdp", None),
        P("section", None),
        P("section", "fsdp", None),
        P("section", None),
        P("section", None),
        P("section", None),
        P("section", "fsdp", None),
        P("section", None),
        P("section", "fsdp", None),
        P("section", None),
        P("section", None, None),
        P(),
        P(),
    )
    out_specs = (
        P("section", ("fsdp", "replica"), None, None),
        P("section", ("fsdp", "replica"), None, None),
        P("section", None),
        P("section", None),
        P("section", "fsdp", None),
        P("section", None),
        P("section", "fsdp", None),
        P("section", None),
        P("section", None),
        P("section", None),
        P("section", "fsdp", None),
        P("section", None),
        P("section", "fsdp", None),
        P("section", None),
        P("section", None, None),
    )
    return jax.shard_map(
        on_device, mesh=mesh, in_specs=in_specs, out_specs=out_specs, check_vma=False
    )
```

profile of v0, /device:TPU:0, one launch (start us, length us, event | category | flops | bytes accessed | tf_op | source)
XLA Modules:
  0.0 791.4 jit_solution(12195740200517624447)
XLA Ops:
  16.2 14.6 %all_gather.9 = bf16[1,512,512]{2,1,0:T(8,128)(2,1)S(1)} all-gather(bf16[1,128,512]{2,1,0:T(8,128)(2,1)S(1)} %copy-done.97), channel_id=1, replica_groups=mesh['section'=2,'fsdp'=4,'replica'=4] {'fsdp'}, dimensions={1}, use_global_device_ids=true | all-gather | bytes 655360 | tf_op jit(solution)/shard_map/all_gather | solution.py:226
  30.9 15.5 %all-gather.4.cloned.1.call-done = bf16[1,512,1536]{2,1,0:T(8,128)(2,1)} async-done(((bf16[1,128,1536]{2,1,0:T(8,128)(2,1)}), bf16[1,512,1536]{2,1,0:T(8,128)(2,1)}) %all-gather.4.cloned.1.call-update) | async-done | bytes 1572880 | tf_op jit(solution)/shard_map/all_gather | solution.py:225
  49.7 6.0 reshape.811
  55.8 7.5 copy.360
  63.3 4.5 fusion.273
  67.8 5.3 copy.361
  73.1 4.2 fusion.521
  88.5 6.2 fusion.298
  94.7 26.1 %all-gather.8.cloned.1.call-done = bf16[1,2048,512]{2,1,0:T(8,128)(2,1)} async-done(((bf16[1,512,512]{2,1,0:T(8,128)(2,1)}), bf16[1,2048,512]{2,1,0:T(8,128)(2,1)}) %all-gather.8.cloned.1.call-update) | async-done | bytes 2097168 | tf_op jit(solution)/shard_map/all_gather | solution.py:228
  120.8 11.4 %fusion.250 = bf16[2,196,512]{2,1,0:T(8,128)(2,1)} fusion(f32[2,196,512]{2,1,0:T(8,128)S(1)} %get-tuple-element.163, bf16[1,2048,512]{2,1,0:T(8,128)(2,1)} %all-gather.8.cloned.1.call-done, f32[2,196,2048]{2,1,0:T(8,128)} %get-tuple-element.214, u8[196,2048]{1,0:T(8,128)(4,1)} %get-tuple-element.80, u8[196,2048]{1,0:T(8,128)(4,1)S(1)} %get-tuple-element.79, ...), kind=kOutput, calls=%fused_computation.301 | convolution fusion | flops 878882816 | bytes 7317504 | tf_op jit(solution)/shard_map/dot_general | solution.py:92
  140.6 3.5 fusion.58
  144.1 5.9 reshape.814
  150.0 7.5 copy.379
  157.5 4.5 fusion.272
  162.0 5.2 copy.380
  167.2 4.1 fusion.522
  181.5 3.8 fusion.299
  185.3 7.9 fusion.245
  203.2 5.6 broadcast_select_fusion.6
  208.8 5.9 reshape.817
  214.6 7.5 copy.395
  222.1 4.5 fusion.271
  226.6 5.3 copy.396
  231.9 4.3 fusion.523
  236.2 7.5 fusion.507
  243.8 3.9 bitcast_select_fusion.1
  258.9 13.0 %fusion.297 = (u8[196,2048]{1,0:T(8,128)(4,1)}, f32[2,196,2048]{2,1,0:T(8,128)}, u8[196,2048]{1,0:T(8,128)(4,1)}, f32[2,196,2048]{2,1,0:T(8,128)}, u8[196,2048]{...) fusion(f32[2,196,2048]{2,1,0:T(8,128)} %copy-done.131, ...), kind=kOutput, calls=%fused_computation.435 | convolution fusion | flops 851587072 | bytes 24190016 | tf_op jit(solution)/shard_map/dot_general | solution.py:90
  271.9 7.1 fusion.17
  292.7 5.9 reshape.820
  298.6 7.5 copy.407
  306.0 4.2 fusion.270
  310.2 5.4 copy.418
  315.7 6.6 convert_reduce_fusion.8
  327.6 7.4 copy.528
  335.1 7.3 reshape.822
  351.9 8.2 %fusion.18 = f32[2,196,2048]{2,1,0:T(8,128)} fusion(f32[2,196,2048]{2,1,0:T(8,128)S(1)} %copy-done.17, u8[196,2048]{1,0:T(8,128)(4,1)S(1)} %copy-done.94), kind=kLoop, calls=%fused_computation.34 | loop fusion | flops 52183040 | bytes 6823936 | tf_op jit(solution)/shard_map/jvp()/erfc | solution.py:97
  360.2 7.9 fusion.19
  369.2 5.3 copy.479
  375.4 4.4 reshape.819
  379.8 7.6 copy.405
  387.4 4.4 reshape.825
  391.8 7.5 copy.451
  399.3 5.6 convert_element_type.435
  422.1 5.6 convert_reduce_fusion.4
  437.4 4.2 fusion.269
  441.6 5.6 copy.439
  447.2 6.6 convert_reduce_fusion.7
  458.6 7.4 copy.530
  466.0 7.3 reshape.824
  481.2 5.3 copy.484
  492.0 4.7 convert_element_type.437
  516.0 4.2 fusion.268
  520.2 5.5 copy.461
  525.7 6.6 convert_reduce_fusion.6
  537.1 7.4 copy.534
  544.5 7.3 reshape.827
  564.1 5.3 copy.489
  570.7 5.5 convert_element_type.439
  576.2 4.7 fusion.60
  588.8 4.4 fusion.117
  599.8 10.4 %fusion.260 = bf16[1,2,196,512]{3,2,1,0:T(8,128)(2,1)S(1)} fusion(f32[2,196,512]{2,1,0:T(8,128)S(1)} %copy-done.41, bf16[1,2048,512]{2,1,0:T(8,128)(2,1)} %all-gather.8.cloned.1.call-done, f32[2,196,2048]{2,1,0:T(8,128)} %get-tuple-element.220, u8[196,2048]{1,0:T(8,128)(4,1)S(1)} %copy-done.132, u8[196,2048]{1,0:T(8,128)(4,1)S(1)} %copy-done.133, ...), kind=kOutput, calls=%fused_computation.313 | convolution fusion | flops 878882816 | bytes 7317504 | tf_op jit(solution)/shard_map/dot_general | solution.py:92
  629.6 29.9 %reduce-scatter.9.cloned.1.call-done = bf16[1,128,2048]{2,1,0:T(8,128)(2,1)} async-done(((bf16[1,512,2048]{2,1,0:T(8,128)(2,1)}), bf16[1,128,2048]{2,1,0:T(8,128)(2,1)}) %reduce-scatter.9.cloned.1.call-update) | async-done | bytes 524304 | tf_op jit(solution)/shard_map/reduce_scatter | solution.py:304
  659.5 38.2 %reduce-scatter.11.cloned.1.call-done = bf16[1,512,512]{2,1,0:T(8,128)(2,1)} async-done(((bf16[1,2048,512]{2,1,0:T(8,128)(2,1)}), bf16[1,512,512]{2,1,0:T(8,128)(2,1)}) %reduce-scatter.11.cloned.1.call-update) | async-done | bytes 524304 | tf_op jit(solution)/shard_map/reduce_scatter | solution.py:307
  697.9 79.5 %all-reduce = (f32[1,512]{1,0:T(1,128)}, f32[1,512]{1,0:T(1,128)}, f32[1,1536]{1,0:T(1,128)}, f32[1,512]{1,0:T(1,128)}, f32[1,512]{1,0:T(1,128)}, /*index=5*/f32...) all-reduce(f32[1,512]{1,0:T(1,128)S(1)} %bitcast.584, ...), channel_id=1, replica_groups=mesh['section'=2,'fsdp'=4,'replica'=4] {'fsdp','replica'}, use_global_device_ids=true, to_apply=%region_48.49 | all-reduce | flops 9360 | bytes 74880 | tf_op jit(solution)/shard_map/psum | solution.py:317
  (540 shorter events, 215.5 us)
Async XLA Ops:
  7.2 7.4 copy-start
  7.2 39.2 %all-gather.4.cloned.1.call-start = ((), (), s32[]{:S(2)}) async-start(), calls=%async_computation.4 | async-start | bytes 1966080 | tf_op jit(solution)/shard_map/all_gather | solution.py:225
  8.0 80.5 %all-gather.6.cloned.1.call-start = ((), (), s32[]{:S(2)}) async-start(), calls=%async_computation.5 | async-start | bytes 2621440 | tf_op jit(solution)/shard_map/all_gather | solution.py:227
  8.7 112.0 %all-gather.8.cloned.1.call-start = ((), (), s32[]{:S(2)}) async-start(), calls=%async_computation.6 | async-start | bytes 2621440 | tf_op jit(solution)/shard_map/all_gather | solution.py:228
  9.4 620.2 %reduce-scatter.7.cloned.1.call-start = ((), (), s32[]{:S(2)}) async-start(), calls=%async_computation.8 | async-start | bytes 655360 | tf_op jit(solution)/shard_map/reduce_scatter | solution.py:301
  13.3 17.4 %copy-start.112 = (f32[1,1536]{1,0:T(1,128)S(1)}, f32[1,1536]{1,0:T(1,128)}, u32[]{:S(2)}) copy-start(f32[1,1536]{1,0:T(1,128)} %param.22) | copy-start | bytes 18436
  16.1 151.1 %copy-start.51 = (f32[16,49,49]{2,0,1:T(8,128)}, f32[16,49,49]{2,0,1:T(8,128)S(1)}, u32[]{:S(2)}) copy-start(f32[16,49,49]{2,0,1:T(8,128)S(1)} %copy.362) | copy-start | bytes 460996
  73.0 94.2 %copy-start.66 = (f32[2,4,49,49]{3,2,1,0:T(8,128)}, f32[2,4,49,49]{3,2,1,0:T(8,128)S(1)}, u32[]{:S(2)}) copy-start(f32[2,4,49,49]{3,2,1,0:T(8,128)S(1)} %add.493) | copy-start | bytes 230500
  88.5 32.3 %copy-start.126 = (f32[1,512]{1,0:T(1,128)S(1)}, f32[1,512]{1,0:T(1,128)}, u32[]{:S(2)}) copy-start(f32[1,512]{1,0:T(1,128)} %param.30) | copy-start | bytes 6148
  132.2 3.3 collective-permute-start
  135.5 44.3 %copy-start.23 = (bf16[2,196,512]{2,1,0:T(8,128)(2,1)}, bf16[2,196,512]{2,1,0:T(8,128)(2,1)S(1)}, u32[]{:S(2)}) copy-start(bf16[2,196,512]{2,1,0:T(8,128)(2,1)S(1)} %collective-permute-done) | copy-start | bytes 1204228
  185.3 7.9 %copy-start.131 = (f32[2,196,2048]{2,1,0:T(8,128)}, f32[2,196,2048]{2,1,0:T(8,128)S(1)}, u32[]{:S(2)}) copy-start(f32[2,196,2048]{2,1,0:T(8,128)S(1)} %get-tuple-element.217) | copy-start | bytes 9633796
  185.3 10.2 %copy-start.89 = (bf16[4,196,512]{2,0,1:T(4,128)(2,1)S(1)}, bf16[4,196,512]{2,0,1:T(4,128)(2,1)}, u32[]{:S(2)}) copy-start(bf16[4,196,512]{2,0,1:T(4,128)(2,1)} %param.18) | copy-start | bytes 2408452
  185.3 11.9 %copy-start.24 = (bf16[2,196,512]{2,1,0:T(8,128)(2,1)S(1)}, bf16[2,196,512]{2,1,0:T(8,128)(2,1)}, u32[]{:S(2)}) copy-start(bf16[2,196,512]{2,1,0:T(8,128)(2,1)} %copy-done.23) | copy-start | bytes 1204228
  193.2 5.9 copy-start.91
  193.2 3.8 collective-permute-start.1
  236.2 7.6 copy-start.26
  236.2 7.6 copy-start.28
  271.9 7.1 copy-start.19
  271.9 7.2 copy-start.69
  271.9 7.2 copy-start.120
  315.7 6.6 copy-start.31
  349.1 11.1 %copy-start.71 = (bf16[2,196,512]{2,0,1:T(2,128)(2,1)}, bf16[2,196,512]{2,0,1:T(2,128)(2,1)S(1)}, u32[]{:S(2)}) copy-start(bf16[2,196,512]{2,0,1:T(2,128)(2,1)S(1)} %copy.475) | copy-start | bytes 1204228
  349.4 18.7 %copy-start.73 = (bf16[2,11,14,512]{3,0,2,1:T(2,128)(2,1)}, bf16[2,11,14,512]{3,0,2,1:T(2,128)(2,1)S(1)}, u32[]{:S(2)}) copy-start(bf16[2,11,14,512]{3,0,2,1:T(2,128)(2,1)S(1)} %slice.394) | copy-start | bytes 946180
  350.6 71.5 %collective-permute-start.2 = (bf16[2,196,512]{2,1,0:T(8,128)(2,1)}, bf16[2,196,512]{2,1,0:T(8,128)(2,1)}, u32[]{:S(2)}, u32[]{:S(2)}) collective-permute-start(bf16[2,196,512]{2,1,0:T(8,128)(2,1)} %add_convert_fusion.11), channel_id=1, source_target_pairs={{16,0},{17,1},{18,2},{19,3},{20,4},{21,5},{22,6},{23,7},{24,8},{25... | collective-permute-start | bytes 1204232 | tf_op jit(solution)/shard_map/ppermute | solution.py:21
  351.9 8.3 %copy-start.9 = (f32[2,196,2048]{2,1,0:T(8,128)S(1)}, f32[2,196,2048]{2,1,0:T(8,128)}, u32[]{:S(2)}) copy-start(f32[2,196,2048]{2,1,0:T(8,128)} %get-tuple-element.144) | copy-start | bytes 9633796
  351.9 8.3 %copy-start.93 = (u8[196,2048]{1,0:T(8,128)(4,1)S(1)}, u8[196,2048]{1,0:T(8,128)(4,1)}, u32[]{:S(2)}) copy-start(u8[196,2048]{1,0:T(8,128)(4,1)} %get-tuple-element.143) | copy-start | bytes 1204228
  360.2 9.0 %copy-start.6 = (bf16[8,49,3,16,32]{1,4,3,0,2:T(8,128)(2,1)S(1)}, bf16[8,49,3,16,32]{1,4,3,0,2:T(8,128)(2,1)}, u32[]{:S(2)}) copy-start(bf16[8,49,3,16,32]{1,4,3,0,2:T(8,128)(2,1)} %get-tuple-element.132) | copy-start | bytes 3612676
  369.2 5.3 copy-start.59
  369.2 6.2 copy-start.54
  379.8 7.6 copy-start.53
  399.3 11.4 %copy-start.56 = (bf16[8,49,16,32]{1,3,2,0:T(8,128)(2,1)S(1)}, bf16[8,49,16,32]{1,3,2,0:T(8,128)(2,1)}, u32[]{:S(2)}) copy-start(bf16[8,49,16,32]{1,3,2,0:T(8,128)(2,1)} %get-tuple-element.180) | copy-start | bytes 1204228
  404.9 10.1 %copy-start.55 = (bf16[8,49,16,32]{1,3,2,0:T(8,128)(2,1)S(1)}, bf16[8,49,16,32]{1,3,2,0:T(8,128)(2,1)}, u32[]{:S(2)}) copy-start(bf16[8,49,16,32]{1,3,2,0:T(8,128)(2,1)} %get-tuple-element.178) | copy-start | bytes 1204228
  415.6 6.4 copy-start.67
  422.1 5.7 copy-start.37
  422.1 5.7 copy-start.123
  447.2 6.6 copy-start.30
  481.2 5.3 copy-start.61
  481.2 6.2 copy-start.84
  481.2 8.5 %copy-start.72 = (bf16[2,196,512]{2,0,1:T(2,128)(2,1)S(1)}, bf16[2,196,512]{2,0,1:T(2,128)(2,1)}, u32[]{:S(2)}) copy-start(bf16[2,196,512]{2,0,1:T(2,128)(2,1)} %copy-done.71) | copy-start | bytes 1204228
  487.4 16.3 %collective-permute-start.3 = (bf16[2,196,512]{2,1,0:T(8,128)(2,1)S(1)}, bf16[2,196,512]{2,1,0:T(8,128)(2,1)S(1)}, u32[]{:S(2)}, u32[]{:S(2)}) collective-permute-start(bf16[2,196,512]{2,1,0:T(8,128)(2,1)S(1)} %copy-done.84), channel_id=1, source_target_pairs={{16,0},{17,1},{18,2},{19,3},{20,4},{21,5},{22,6},{23,7},{24,8},{25... | collective-permute-start | bytes 1204232 | tf_op jit(solution)/shard_map/ppermute | solution.py:21
  525.7 6.6 copy-start.29
  555.9 5.7 copy-start.14
  560.7 68.9 %reduce-scatter.5.cloned.1.call-start = ((), (), s32[]{:S(2)}) async-start(), calls=%async_computation.7 | async-start | bytes 1966080 | tf_op jit(solution)/shard_map/reduce_scatter | solution.py:298
  581.0 78.6 %reduce-scatter.9.cloned.1.call-start = ((), (), s32[]{:S(2)}) async-start(), calls=%async_computation.9 | async-start | bytes 2621440 | tf_op jit(solution)/shard_map/reduce_scatter | solution.py:304
  588.7 109.0 %reduce-scatter.11.cloned.1.call-start = ((), (), s32[]{:S(2)}) async-start(), calls=%async_computation.10 | async-start | bytes 2621440 | tf_op jit(solution)/shard_map/reduce_scatter | solution.py:307
  599.5 177.9 %all-reduce.4.cloned.1.call-start = ((), (), s32[]{:S(2)}) async-start(), calls=%async_computation.11 | async-start | bytes 3145728 | tf_op jit(solution)/shard_map/psum | solution.py:312
  599.8 10.4 %copy-start.92 = (bf16[2,196,512]{2,1,0:T(8,128)(2,1)S(1)}, bf16[2,196,512]{2,1,0:T(8,128)(2,1)}, u32[]{:S(2)}) copy-start(bf16[2,196,512]{2,1,0:T(8,128)(2,1)} %copy-done.91) | copy-start | bytes 1204228
  610.3 9.2 %copy-start.104 = (s32[2401]{0:T(1024)S(1)}, s32[2401]{0:T(1024)}, u32[]{:S(2)}) copy-start(s32[2401]{0:T(1024)} %copy-done.103) | copy-start | bytes 28816
  610.3 11.0 %copy-start.47 = (f32[2,14,14,512]{3,0,2,1:T(2,128)S(1)}, f32[2,14,14,512]{3,0,2,1:T(2,128)}, u32[]{:S(2)}) copy-start(f32[2,14,14,512]{3,0,2,1:T(2,128)} %copy-done.46) | copy-start | bytes 2408452
  613.7 10.0 %copy-start.40 = (f32[2,196,512]{2,1,0:T(8,128)S(1)}, f32[2,196,512]{2,1,0:T(8,128)}, u32[]{:S(2)}) copy-start(f32[2,196,512]{2,1,0:T(8,128)} %copy-done.39) | copy-start | bytes 2408452
  613.7 10.0 %copy-start.43 = (f32[2,196,512]{2,1,0:T(8,128)S(1)}, f32[2,196,512]{2,1,0:T(8,128)}, u32[]{:S(2)}) copy-start(f32[2,196,512]{2,1,0:T(8,128)} %copy-done.42) | copy-start | bytes 2408452
  626.7 71.0 %copy-start.107 = (f32[512]{0:T(512)S(1)}, f32[512]{0:T(512)}, u32[]{:S(2)}) copy-start(f32[512]{0:T(512)} %get-tuple-element.87) | copy-start | bytes 6148
  626.7 71.1 %copy-start.106 = (f32[512]{0:T(512)S(1)}, f32[512]{0:T(512)}, u32[]{:S(2)}) copy-start(f32[512]{0:T(512)} %get-tuple-element.125) | copy-start | bytes 6148
  626.7 71.1 %copy-start.105 = (f32[512]{0:T(512)S(1)}, f32[512]{0:T(512)}, u32[]{:S(2)}) copy-start(f32[512]{0:T(512)} %get-tuple-element.83) | copy-start | bytes 6148
  626.7 71.1 %copy-start.113 = (f32[512]{0:T(512)S(1)}, f32[512]{0:T(512)}, u32[]{:S(2)}) copy-start(f32[512]{0:T(512)} %get-tuple-element.103) | copy-start | bytes 6148
  626.7 71.1 %copy-start.114 = (f32[512]{0:T(512)S(1)}, f32[512]{0:T(512)}, u32[]{:S(2)}) copy-start(f32[512]{0:T(512)} %get-tuple-element.104) | copy-start | bytes 6148
  626.7 71.1 %copy-start.115 = (f32[512]{0:T(512)S(1)}, f32[512]{0:T(512)}, u32[]{:S(2)}) copy-start(f32[512]{0:T(512)} %get-tuple-element.105) | copy-start | bytes 6148
  626.7 71.1 %copy-start.109 = (f32[512]{0:T(512)S(1)}, f32[512]{0:T(512)}, u32[]{:S(2)}) copy-start(f32[512]{0:T(512)} %get-tuple-element.198) | copy-start | bytes 6148
  626.8 71.1 %copy-start.110 = (f32[512]{0:T(512)S(1)}, f32[512]{0:T(512)}, u32[]{:S(2)}) copy-start(f32[512]{0:T(512)} %get-tuple-element.186) | copy-start | bytes 6148
  626.8 71.1 %copy-start.111 = (f32[512]{0:T(512)S(1)}, f32[512]{0:T(512)}, u32[]{:S(2)}) copy-start(f32[512]{0:T(512)} %get-tuple-element.196) | copy-start | bytes 6148
  626.8 71.1 %copy-start.108 = (f32[2048]{0:T(1024)S(1)}, f32[2048]{0:T(1024)}, u32[]{:S(2)}) copy-start(f32[2048]{0:T(1024)} %get-tuple-element.227) | copy-start | bytes 24580
  629.3 155.0 %copy-start.1 = (f32[1,169,16]{1,2,0:T(8,128)S(1)}, f32[1,169,16]{1,2,0:T(8,128)}, u32[]{:S(2)}) copy-start(f32[1,169,16]{1,2,0:T(8,128)} %param.31) | copy-start | bytes 32452
  777.4 5.8 copy-start.90
  (82 other events, 239.8 us)
Sparse Core Ops, SparseCore 0:
  9.9 36.4 all-gather.3
  48.2 35.2 all-gather.5
  85.4 35.3 all-gather.7
  560.8 26.3 reduce-scatter.6
  590.3 30.9 reduce-scatter.4
  624.3 35.1 reduce-scatter.8
  662.5 35.1 reduce-scatter.10
  700.5 72.1 all-reduce.3
where the time goes:
time: 801 us; the launch traced here: 791 us
  local copies, waits for them, and re-layouts  255 us (32%)
  matrix products  178 us (22%)
  other arithmetic  126 us (16%)
  waiting for transfers between devices  113 us (14%)
  blocking collectives  94.1 us (12%)
  between operations  16.9 us (2%)
    psum x1, blocking collectives, on_device(): lax.psum((minor_total[0], minor_total[1], minor_total[2], minor_total[3],...  79.5 us
    reshape x12, local copies, waits for them, and re-layouts, split_heads(): packed.reshape(-1, WIN * WIN, 3, HEADS, HEAD_DIM).transpose(2, 0, 3, 1, 4)  77.4 us
    convert_element_type x9, local copies, waits for them, and re-layouts, backward_layer(): grad_packed = jnp.stack([grad_query, grad_keys, grad_values], 2).reshape(...  60.1 us
    reduce_scatter x1, waiting for transfers between devices, on_device(): lax.psum_scatter(large_total[3][None].astype(jnp.bfloat16), 'fsdp', scatt...  38.2 us
    dot_general x12, matrix products, row_product(): jnp.einsum('ri,rj->ij', left.reshape(-1, left.shape[-1]), right.reshape(-...  34 us
    reduce_scatter x1, waiting for transfers between devices, on_device(): lax.psum_scatter(large_total[2][None].astype(jnp.bfloat16), 'fsdp', scatt...  29.9 us
    dot_general x3, matrix products, forward_layer(): jnp.dot(activated, w_fc2, preferred_element_type=jnp.float32) + bias_fc2  29.7 us
    all_gather x1, waiting for transfers between devices, fetch_forward(): lax.all_gather(fc2_weight, 'fsdp', axis=1, tiled=True)  26.1 us
  transfers between devices with their start and end apart: 12, of which 5 were waited for; matrix products, arithmetic and copies ran while one was open for 26% of the time, Pallas kernels for 0%

commit v1 on v0

v1 whole, which is shorter than its diff:
```python
import functools

import jax
import jax.numpy as jnp
import numpy as np
from jax import lax
from jax.experimental import pallas as pl
from jax.experimental.pallas import tpu as pltpu
from jax.sharding import PartitionSpec as P

D = 512
HEADS = 16
HEAD_DIM = 32
FF = 2048
WIN = 7
SHIFT = 3
SIDE = 14
REL = 169
TOKENS = SIDE * SIDE
SPOTS = WIN * WIN
PAD = 64
ACROSS = SIDE // WIN
WINDOWS = ACROSS * ACROSS
ROWS = WINDOWS * PAD
HALVES = 2
HALF_HEADS = HEADS // HALVES
HALF = HALF_HEADS * HEAD_DIM
WIDE = HALF_HEADS * PAD
SCALE = HEAD_DIM ** (-0.5)
FAR = -1e30
CHUNK = 512
VMEM = 56 * 2**20
F32 = jnp.float32
BF16 = jnp.bfloat16

NT = (((1,), (1,)), ((), ()))
TN = (((0,), (0,)), ((), ()))


def dot(left, right):
    return jnp.dot(left, right, preferred_element_type=F32)


def dot_nt(left, right):
    return lax.dot_general(left, right, NT, preferred_element_type=F32)


def dot_tn(left, right):
    return lax.dot_general(left, right, TN, preferred_element_type=F32)


def window_tokens(shift):
    tokens = np.full((ROWS,), -1, np.int32)
    for row in range(ROWS):
        window, spot = divmod(row, PAD)
        if spot < SPOTS:
            down = window // ACROSS * WIN + spot // WIN
            right = window % ACROSS * WIN + spot % WIN
            tokens[row] = (down + shift) % SIDE * SIDE + (right + shift) % SIDE
    return tokens


def placement(shift):
    return (window_tokens(shift)[:, None] == np.arange(TOKENS)[None, :]).astype(np.float32)


def head_mask():
    rows = lax.broadcasted_iota(jnp.int32, (WIDE, HALF), 0) // PAD
    columns = lax.broadcasted_iota(jnp.int32, (WIDE, HALF), 1) // HEAD_DIM
    return (rows == columns).astype(F32).astype(BF16)


def spread(block, mask):
    return jnp.concatenate([block] * HALF_HEADS, 0) * mask


def gather_heads(block, mask):
    kept = (block * mask.astype(F32)).reshape(HALF_HEADS, PAD, HALF)
    return jnp.sum(kept, 0)


def by_head(values, reduce, neutral):
    parts = []
    for start in range(0, values.shape[1], 2 * PAD):
        tile = values[:, start : start + 2 * PAD]
        low = lax.broadcasted_iota(jnp.int32, tile.shape, 1) < PAD
        early = reduce(jnp.where(low, tile, neutral), axis=1, keepdims=True)
        later = reduce(jnp.where(low, neutral, tile), axis=1, keepdims=True)
        parts.append(jnp.where(low, early, later))
    return jnp.concatenate(parts, 1)


def norm_stats(values):
    centre = values - jnp.mean(values, -1, keepdims=True)
    inverse = lax.rsqrt(jnp.mean(centre * centre, -1, keepdims=True) + 1e-05)
    return centre * inverse, inverse


def norm_back(grad, unit, inverse, gain):
    scaled = grad * gain
    inner = jnp.mean(scaled * unit, -1, keepdims=True)
    return inverse * (scaled - jnp.mean(scaled, -1, keepdims=True) - unit * inner)


def column_sum(values):
    return jnp.sum(values, 0, keepdims=True)


def attention_forward(
    x_ref, place_ref, wqkv_ref, wproj_ref, gain_ref, shift_ref, bqkv_ref, bproj_ref, bias_ref,
    normed_ref, packed_ref, probs_ref, attended_ref, middle_ref,
):
    count = x_ref.shape[0]
    for image in range(count):
        rows = pl.ds(image * ROWS, ROWS)
        field = dot(place_ref[...], x_ref[image])
        unit, _ = norm_stats(field)
        normed = (unit * gain_ref[...] + shift_ref[...]).astype(BF16)
        normed_ref[rows, :] = normed
        middle_ref[rows, :] = field
        packed_ref[rows, :] = (dot(normed, wqkv_ref[...]) + bqkv_ref[...]).astype(BF16)
    mask = head_mask()

    def window(index, carry):
        rows = pl.ds(pl.multiple_of(index * PAD, PAD), PAD)
        which = lax.rem(index, bias_ref.shape[0])
        for half in range(HALVES):
            columns = pl.ds(half * HALF, HALF)
            query = packed_ref[rows, columns]
            keys = spread(packed_ref[rows, pl.ds(D + half * HALF, HALF)], mask)
            values = spread(packed_ref[rows, pl.ds(2 * D + half * HALF, HALF)], mask)
            wide = pl.ds(half * WIDE, WIDE)
            scores = dot_nt(query, keys) * SCALE + bias_ref[which, :, wide]
            grown = jnp.exp(scores - by_head(scores, jnp.max, FAR))
            probs = grown / by_head(grown, jnp.sum, 0.0)
            probs_ref[rows, wide] = probs
            attended_ref[rows, columns] = dot(probs.astype(BF16), values).astype(BF16)
        return carry

    lax.fori_loop(0, count * WINDOWS, window, 0)
    for image in range(count):
        rows = pl.ds(image * ROWS, ROWS)
        middle_ref[rows, :] += dot(attended_ref[rows, :], wproj_ref[...]) + bproj_ref[...]


def feed_forward(
    middle_ref, back_ref, wfc1_ref, wfc2_ref, gain_ref, shift_ref, bfc1_ref, bfc2_ref,
    out_ref, normed_ref, activated_ref, slope_ref,
):
    for image in range(out_ref.shape[0]):
        rows = pl.ds(image * ROWS, ROWS)
        middle = middle_ref[rows, :]
        unit, _ = norm_stats(middle)
        normed = (unit * gain_ref[...] + shift_ref[...]).astype(BF16)
        normed_ref[rows, :] = normed
        for start in range(0, FF, CHUNK):
            columns = pl.ds(start, CHUNK)
            hidden = dot(normed, wfc1_ref[:, columns]) + bfc1_ref[:, columns]
            area = 0.5 * (1.0 + lax.erf(hidden * (0.5**0.5)))
            height = jnp.exp(-0.5 * hidden * hidden) * ((0.5 / np.pi) ** 0.5)
            activated_ref[rows, columns] = (hidden * area).astype(BF16)
            slope_ref[rows, columns] = (area + hidden * height).astype(BF16)
        result = middle + (dot(activated_ref[rows, :], wfc2_ref[...]) + bfc2_ref[...])
        out_ref[image] = dot(back_ref[...], result.astype(BF16)).astype(BF16)


def feed_backward(
    g_ref, place_ref, normed_ref, activated_ref, slope_ref, middle_ref, wfc1_ref, wfc2_ref, gain_ref,
    gfc1_ref, gfc2_ref, gmid_ref, gbfc1_ref, gbfc2_ref, ggain_ref, gshift_ref,
    gm_ref, gh_ref,
):
    count = g_ref.shape[0]
    gbfc1 = gbfc2 = ggain = gshift = 0.0
    for image in range(count):
        rows = pl.ds(image * ROWS, ROWS)
        incoming = dot(place_ref[...], g_ref[image])
        gm = incoming.astype(BF16)
        gm_ref[rows, :] = gm
        gbfc2 = gbfc2 + column_sum(incoming)
        sums = []
        for start in range(0, FF, CHUNK):
            columns = pl.ds(start, CHUNK)
            grad = dot_nt(gm, wfc2_ref[columns, :])
            gh = (grad * slope_ref[rows, columns].astype(F32)).astype(BF16)
            gh_ref[rows, columns] = gh
            sums.append(column_sum(gh.astype(F32)))
        gbfc1 = gbfc1 + jnp.concatenate(sums, 1)
        grad = dot_nt(gh_ref[rows, :], wfc1_ref[...])
        unit, inverse = norm_stats(middle_ref[rows, :])
        ggain = ggain + column_sum(grad * unit)
        gshift = gshift + column_sum(grad)
        gmid_ref[rows, :] = incoming + norm_back(grad, unit, inverse, gain_ref[...])
    gbfc1_ref[...] = gbfc1
    gbfc2_ref[...] = gbfc2
    ggain_ref[...] = ggain
    gshift_ref[...] = gshift
    for start in range(0, FF, CHUNK):
        columns = pl.ds(start, CHUNK)
        gfc2_ref[columns, :] = dot_tn(activated_ref[:, columns], gm_ref[...]).astype(BF16)
        gfc1_ref[:, columns] = dot_tn(normed_ref[...], gh_ref[:, columns]).astype(BF16)


def attention_backward(
    x_ref, place_ref, back_ref, gmid_ref, probs_ref, packed_ref, attended_ref, normed_ref,
    wqkv_ref, wproj_ref, gain_ref,
    gqkv_ref, gproj_ref, gin_ref, gbqkv_ref, gbproj_ref, ggain_ref, gshift_ref, gbias_ref,
    gb_ref, ga_ref, gpack_ref,
):
    count = x_ref.shape[0]
    gbproj = 0.0
    for image in range(count):
        rows = pl.ds(image * ROWS, ROWS)
        gb = gmid_ref[rows, :].astype(BF16)
        gb_ref[rows, :] = gb
        gbproj = gbproj + column_sum(gb.astype(F32))
        ga_ref[rows, :] = dot_nt(gb, wproj_ref[...]).astype(BF16)
    gbproj_ref[...] = gbproj
    gproj_ref[...] = dot_tn(attended_ref[...], gb_ref[...]).astype(BF16)
    mask = head_mask()
    gbias_ref[...] = jnp.zeros_like(gbias_ref)

    def window(index, carry):
        rows = pl.ds(pl.multiple_of(index * PAD, PAD), PAD)
        for half in range(HALVES):
            columns = pl.ds(half * HALF, HALF)
            key_columns = pl.ds(D + half * HALF, HALF)
            value_columns = pl.ds(2 * D + half * HALF, HALF)
            wide = pl.ds(half * WIDE, WIDE)
            query = packed_ref[rows, columns]
            keys = spread(packed_ref[rows, key_columns], mask)
            values = spread(packed_ref[rows, value_columns], mask)
            probs = probs_ref[rows, wide]
            ga = ga_ref[rows, columns]
            gp = dot_nt(ga, values)
            gs = (probs * (gp - by_head(gp * probs, jnp.sum, 0.0))).astype(BF16)
            gbias_ref[:, wide] += gs.astype(F32)
            gq = dot(gs, keys) * SCALE
            gk = gather_heads(dot_tn(gs, query), mask) * SCALE
            gv = gather_heads(dot_tn(probs.astype(BF16), ga), mask)
            gpack_ref[rows, columns] = gq.astype(BF16)
            gpack_ref[rows, key_columns] = gk.astype(BF16)
            gpack_ref[rows, value_columns] = gv.astype(BF16)
        return carry

    lax.fori_loop(0, count * WINDOWS, window, 0)
    gqkv_ref[...] = dot_tn(normed_ref[...], gpack_ref[...]).astype(BF16)
    gbqkv = ggain = gshift = 0.0
    for image in range(count):
        rows = pl.ds(image * ROWS, ROWS)
        gpack = gpack_ref[rows, :]
        gbqkv = gbqkv + column_sum(gpack.astype(F32))
        grad = dot_nt(gpack, wqkv_ref[...])
        unit, inverse = norm_stats(dot(place_ref[...], x_ref[image]))
        ggain = ggain + column_sum(grad * unit)
        gshift = gshift + column_sum(grad)
        gin = gmid_ref[rows, :] + norm_back(grad, unit, inverse, gain_ref[...])
        gin_ref[image] = dot(back_ref[...], gin.astype(BF16)).astype(BF16)
    gbqkv_ref[...] = gbqkv
    ggain_ref[...] = ggain
    gshift_ref[...] = gshift


def whole(array):
    return pl.BlockSpec(array.shape, lambda step, rank=len(array.shape): (0,) * rank)


def layer_of(array, layer):
    return pl.BlockSpec((array.shape[0] // 2,) + array.shape[1:], lambda step: (layer, 0))


def run(body, operands, outs, layer, weights, scratch=(), flops=0):
    outs = [jax.ShapeDtypeStruct(shape, kind) for shape, kind in outs]
    specs = [layer_of(item, layer) if index in weights else whole(item) for index, item in enumerate(operands)]
    return pl.pallas_call(
        body,
        grid=(1,),
        out_shape=outs,
        in_specs=specs,
        out_specs=[whole(item) for item in outs],
        scratch_shapes=list(scratch),
        cost_estimate=pl.CostEstimate(flops=flops, bytes_accessed=2**24, transcendentals=0),
        compiler_params=pltpu.CompilerParams(vmem_limit_bytes=VMEM),
    )(*operands)


def fetch_body(depth, *refs):
    count = (len(refs) - 5) // 2
    ins, outs = refs[:count], refs[count : 2 * count]
    far_send, far_recv, near_send, near_recv, local = refs[2 * count :]
    section, mine, replica = (lax.axis_index(name) for name in ("section", "fsdp", "replica"))
    sibling = (1 - section, mine, replica)
    peers = [(section, lax.rem(mine + step, depth), replica) for step in range(1, depth)]
    barrier = pltpu.get_barrier_semaphore()
    for device in peers + [sibling]:
        pl.semaphore_signal(barrier, inc=1, device_id=device, device_id_type=pl.DeviceIdType.MESH)
    pl.semaphore_wait(barrier, depth)

    def slot(item, owner):
        rows = ins[item].shape[0]
        start = pl.multiple_of((section * depth + owner) * rows, rows)
        return outs[item].at[pl.ds(start, rows)]

    def send(source, item, owner, device, leave, arrive):
        copy = pltpu.make_async_remote_copy(
            src_ref=source,
            dst_ref=slot(item, owner),
            send_sem=leave,
            recv_sem=arrive,
            device_id=device,
            device_id_type=pl.DeviceIdType.MESH,
        )
        copy.start()
        return copy

    far, near, kept = [], [], []
    for item in range(count):
        far.append([
            send(ins[item], item, mine, peers[step], far_send.at[item, step], far_recv.at[item, step])
            for step in range(depth - 1)
        ])
    for item in range(count):
        near.append(send(ins[item], item, mine, sibling, near_send.at[item, 0], near_recv.at[item, 0]))
        copy = pltpu.make_async_copy(ins[item], slot(item, mine), local.at[item])
        copy.start()
        kept.append(copy)
    for item in range(count):
        for step in range(1, depth):
            far[item][step - 1].wait_recv()
            owner = lax.rem(mine - step + depth, depth)
            near.append(
                send(slot(item, owner), item, owner, sibling, near_send.at[item, step], near_recv.at[item, step])
            )
    for item in range(count):
        for copy in far[item]:
            copy.wait_send()
        kept[item].wait()
    for copy in near:
        copy.wait()


def fetch(shards):
    depth = lax.axis_size("fsdp")
    count = len(shards)
    outs = [jax.ShapeDtypeStruct((2 * depth * item.shape[0], item.shape[1]), item.dtype) for item in shards]
    return pl.pallas_call(
        functools.partial(fetch_body, depth),
        out_shape=outs,
        in_specs=[pl.BlockSpec(memory_space=pl.ANY)] * count,
        out_specs=[pl.BlockSpec(memory_space=pl.ANY)] * count,
        scratch_shapes=[
            pltpu.SemaphoreType.DMA((count, depth - 1)),
            pltpu.SemaphoreType.DMA((count, depth - 1)),
            pltpu.SemaphoreType.DMA((count, depth)),
            pltpu.SemaphoreType.DMA((count, depth)),
            pltpu.SemaphoreType.DMA((count,)),
        ],
        compiler_params=pltpu.CompilerParams(collective_id=1, has_side_effects=True),
    )(*shards)


def pick(first, early, later):
    return jnp.where(first, early, later)


def on_device(
    images, cotangent, ln1_gain, ln1_bias, qkv_weight, qkv_bias, proj_weight, proj_bias, ln2_gain, ln2_bias,
    fc1_weight, fc1_bias, fc2_weight, fc2_bias, rel_table, rel_index, region,
):
    section = lax.axis_index("section")
    first = section == 0
    halves = lax.axis_size("section")
    count = images.shape[0] // halves
    every = ("section", "fsdp", "replica")
    swap = [(0, 1), (1, 0)]

    small = (ln1_gain, ln1_bias, qkv_bias, proj_bias, ln2_gain, ln2_bias, fc1_bias, fc2_bias, rel_table)
    sizes = [item[0].size for item in small]
    flat = jnp.concatenate([item.reshape(1, -1) for item in small], 1)
    both = lax.all_gather(flat, "section", axis=0, tiled=True)
    params = []
    for layer in range(2):
        pieces, start = [], 0
        for size in sizes:
            pieces.append(both[layer : layer + 1, start : start + size])
            start += size
        params.append(pieces)

    w_qkv, w_proj, w_fc1, w_fc2 = fetch([item[0] for item in (qkv_weight, proj_weight, fc1_weight, fc2_weight)])

    mine_x = lax.dynamic_slice_in_dim(images, section * count, count, 0)
    mine_g = lax.dynamic_slice_in_dim(cotangent, section * count, count, 0)

    edge = PAD - SPOTS
    index = jnp.pad(rel_index, ((0, edge), (0, edge)), constant_values=-1)
    onehot = (index.reshape(-1, 1) == jnp.arange(REL, dtype=jnp.int32)[None, :]).astype(F32)
    tables = jnp.concatenate([params[layer][8].reshape(REL, HEADS) for layer in range(2)], 1)
    spots = jnp.dot(onehot, tables, precision=lax.Precision.HIGHEST)
    spots = spots.reshape(PAD, PAD, 2, HEADS).transpose(2, 0, 3, 1)
    absent = jnp.where(jnp.arange(PAD) < SPOTS, 0.0, FAR).astype(F32)
    spots = spots + absent
    labels = region[np.maximum(window_tokens(0), 0)].reshape(WINDOWS, PAD)
    penalty = jnp.where(labels[:, :, None] != labels[:, None, :], -100.0, 0.0).astype(F32)
    biases = [
        spots[0].reshape(1, PAD, HEADS * PAD),
        (spots[1][None] + penalty[:, :, None, :]).reshape(WINDOWS, PAD, HEADS * PAD),
    ]

    places = [jnp.asarray(placement(shift), BF16) for shift in (0, SHIFT)]
    backs = [jnp.asarray(placement(shift).T, BF16) for shift in (0, SHIFT)]
    rows = count * ROWS
    dense = 2 * rows * D * D

    def forward(x, layer):
        gain_one, shift_one, b_qkv, b_proj, gain_two, shift_two, b_fc1, b_fc2, _ = params[layer]
        normed, packed, probs, attended, middle = run(
            attention_forward,
            (x, places[layer], w_qkv, w_proj, gain_one, shift_one, b_qkv, b_proj, biases[layer]),
            [((rows, D), BF16), ((rows, 3 * D), BF16), ((rows, HEADS * PAD), F32), ((rows, D), BF16), ((rows, D), F32)],
            layer, (2, 3), flops=12 * dense,
        )
        out, normed_two, activated, slope = run(
            feed_forward,
            (middle, backs[layer], w_fc1, w_fc2, gain_two, shift_two, b_fc1, b_fc2),
            [((count, TOKENS, D), BF16), ((rows, D), BF16), ((rows, FF), BF16), ((rows, FF), BF16)],
            layer, (2, 3), flops=12 * dense,
        )
        return out, (x, normed, packed, probs, attended, middle, normed_two, activated, slope)

    def backward(g, kept, layer):
        x, normed, packed, probs, attended, middle, normed_two, activated, slope = kept
        gain_one, gain_two = params[layer][0], params[layer][4]
        row = lambda width: ((1, width), F32)
        gfc1, gfc2, gmid, gbfc1, gbfc2, ggain2, gshift2 = run(
            feed_backward,
            (g, places[layer], normed_two, activated, slope, middle, w_fc1, w_fc2, gain_two),
            [((D, FF), BF16), ((FF, D), BF16), ((rows, D), F32), row(FF), row(D), row(D), row(D)],
            layer, (6, 7),
            (pltpu.VMEM((rows, D), BF16), pltpu.VMEM((rows, FF), BF16)), flops=20 * dense,
        )
        gqkv, gproj, gin, gbqkv, gbproj, ggain1, gshift1, gbias = run(
            attention_backward,
            (x, places[layer], backs[layer], gmid, probs, packed, attended, normed, w_qkv, w_proj, gain_one),
            [((D, 3 * D), BF16), ((D, D), BF16), ((count, TOKENS, D), BF16), row(3 * D), row(D), row(D), row(D),
             ((PAD, HEADS * PAD), F32)],
            layer, (8, 9),
            (pltpu.VMEM((rows, D), BF16), pltpu.VMEM((rows, D), BF16), pltpu.VMEM((rows, 3 * D), BF16)),
            flops=30 * dense,
        )
        gbias = gbias.reshape(PAD, HEADS, PAD).transpose(0, 2, 1).reshape(PAD * PAD, HEADS)
        gtable = jnp.dot(onehot.T, gbias, precision=lax.Precision.HIGHEST)
        minor = (ggain1, gshift1, gbqkv, gbproj, ggain2, gshift2, gbfc1, gbfc2, gtable.reshape(1, -1))
        minor = lax.psum(jnp.concatenate(minor, 1), every)
        owned = [reduce_rows(item) for item in (gfc2, gfc1, gproj, gqkv)]
        return gin, owned[::-1], minor

    def reduce_rows(grad):
        part = lax.psum_scatter(grad, ("fsdp", "section"), scatter_dimension=0, tiled=True)
        part = lax.psum_scatter(part, "replica", scatter_dimension=0, tiled=True)
        return lax.all_gather(part, "replica", axis=0, tiled=True)

    def exchange(early, later):
        other = lax.ppermute(pick(first, later, early), "section", swap)
        own = pick(first, early, later)
        return jnp.concatenate([pick(first, own, other), pick(first, other, own)], 0)

    act_zero, kept_zero = forward(mine_x, 0)
    act_one, kept_one = forward(act_zero, 1)
    gin_one, owned_one, minor_one = backward(mine_g, kept_one, 1)
    gin_zero, owned_zero, minor_zero = backward(gin_one, kept_zero, 0)
    activations = exchange(act_zero, act_one)
    input_grad = exchange(gin_zero, gin_one)
    owned = [exchange(early, later).astype(F32)[None] for early, later in zip(owned_zero, owned_one)]
    minor = pick(first, minor_zero, minor_one)
    minors, start = [], 0
    for size, item in zip(sizes, small):
        minors.append(minor[:, start : start + size].reshape(item.shape))
        start += size
    return (
        activations[None], input_grad[None],
        minors[0], minors[1], owned[0], minors[2], owned[1], minors[3], minors[4], minors[5],
        owned[2], minors[6], owned[3], minors[7], minors[8],
    )


def solution(mesh):
    sliced = P("section", "fsdp", None)
    vector = P("section", None)
    tokens = P(("fsdp", "replica"), None, None)
    in_specs = (
        tokens, tokens, vector, vector, sliced, vector, sliced, vector, vector, vector,
        sliced, vector, sliced, vector, P("section", None, None), P(), P(),
    )
    result = P("section", ("fsdp", "replica"), None, None)
    out_specs = (
        result, result, vector, vector, sliced, vector, sliced, vector, vector, vector,
        sliced, vector, sliced, vector, P("section", None, None),
    )
    return jax.shard_map(on_device, mesh=mesh, in_specs=in_specs, out_specs=out_specs, check_vma=False)
```

time: 801 us -> 733 us (0.915)
  waiting for transfers between devices: 113 us -> 381 us
  local copies, waits for them, and re-layouts: 255 us -> 24.2 us
  Pallas kernels: 0 us -> 176 us
  matrix products: 178 us -> 4.05 us
  other arithmetic: 126 us -> 7.8 us
  blocking collectives: 94.1 us -> 116 us
    reduce_scatter x4 -> x16, waiting for transfers between devices: 68.1 us -> 377 us  [the longest x8 301 us: reduce_rows(): lax.psum_scatter(grad, ('fsdp', 'section'), scatter_dimension=0, tiled=True)]
    pallas_call x0 -> x9, Pallas kernels: none -> 176 us  [the longest x8 99.6 us: run(): pl.pallas_call(body, grid=(1,), out_shape=outs, in_specs=specs, out_specs...]
    dot_general x58 -> x3, matrix products: 178 us -> 4.05 us  [the longest x2 2.79 us: backward(): gtable = jnp.dot(onehot.T, gbias, precision=lax.Precision.HIGHEST)]
    all_gather x1 -> x9, blocking collectives: 14.6 us -> 116 us  [the longest x8 114 us: reduce_rows(): return lax.all_gather(part, 'replica', axis=0, tiled=True)]
    reshape x27 -> x15, local copies, waits for them, and re-layouts: 96.4 us -> 2.09 us  [the longest x6 0.99 us: backward(): gbias.reshape(PAD, HEADS, PAD).transpose(0, 2, 1).reshape(PAD * PAD, HEADS)]
    psum x1 -> x0, blocking collectives: 79.5 us -> none  [on_device(): lax.psum((minor_total[0], minor_total[1], minor_total[2], minor_total[3],...]
    convert_element_type x15 -> x0, local copies, waits for them, and re-layouts: 62 us -> none  [the longest x9 60.1 us: backward_layer(): grad_packed = jnp.stack([grad_query, grad_keys, grad_values], 2).reshape(...]
    all_gather x3 -> x0, waiting for transfers between devices: 41.5 us -> none  [the longest x1 26.1 us: fetch_forward(): lax.all_gather(fc2_weight, 'fsdp', axis=1, tiled=True)]
  transfers between devices with their start and end apart: 12 -> 23, of which waited for: 5 -> 17; matrix products, arithmetic and copies ran while one was open for 26% -> 2% of each run, Pallas kernels for 0% -> 0%
where the time goes in v1:
time: 733 us; the launch traced here: 727 us
  waiting for transfers between devices  381 us (52%)
  Pallas kernels  176 us (24%)
  blocking collectives  116 us (16%)
  local copies, waits for them, and re-layouts  24.2 us (3%)
  between operations  16.7 us (2%)
  other arithmetic  7.8 us (1%)
    reduce_scatter x8, waiting for transfers between devices, reduce_rows(): lax.psum_scatter(grad, ('fsdp', 'section'), scatter_dimension=0, tiled=True)  301 us
    all_gather x8, blocking collectives, reduce_rows(): return lax.all_gather(part, 'replica', axis=0, tiled=True)  114 us
    pallas_call x8, Pallas kernels, run(): pl.pallas_call(body, grid=(1,), out_shape=outs, in_specs=specs, out_specs...  99.6 us
    pallas_call x1, Pallas kernels, fetch(): pl.pallas_call(functools.partial(fetch_body, depth), out_shape=outs, in_s...  76 us
    reduce_scatter x8, waiting for transfers between devices, reduce_rows(): part = lax.psum_scatter(part, 'replica', scatter_dimension=0, tiled=True)  75.8 us
  transfers between devices with their start and end apart: 23, of which 17 were waited for; matrix products, arithmetic and copies ran while one was open for 2% of the time, Pallas kernels for 0%

profile of v1, /device:TPU:0, one launch (start us, length us, event | category | flops | bytes accessed | tf_op | source)
XLA Modules:
  0.0 726.9 jit_solution(15575383631955290154)
XLA Ops:
  8.1 0.7 constant_dynamic-update-slice_fusion.8
  8.8 0.8 copy.68
  9.7 0.7 constant_dynamic-update-slice_fusion.7
  10.4 0.7 constant_dynamic-update-slice_fusion.6
  11.1 0.7 constant_dynamic-update-slice_fusion.5
  11.8 0.7 constant_dynamic-update-slice_fusion.4
  12.5 0.7 constant_dynamic-update-slice_fusion.3
  13.2 0.7 constant_dynamic-update-slice_fusion.2
  13.9 0.7 constant_dynamic-update-slice_fusion.1
  14.6 2.0 all-gather
  18.5 0.7 pad_clamp_fusion
  19.2 1.9 gather_fusion
  21.2 0.8 pad.4
  22.6 1.3 fusion.2
  25.2 0.9 reshape_squeeze.3.bias_ref
  26.4 0.8 constant_dynamic-slice_fusion
  27.2 0.8 copy.84.g_ref
  28.0 0.8 copy.83.x_ref
  29.5 1.1 broadcast_add_fusion.bias_ref
  30.6 76.0 %shard_map.334 = (bf16[1024,1536]{1,0:T(8,128)(2,1)}, bf16[1024,512]{1,0:T(8,128)(2,1)}, bf16[1024,2048]{1,0:T(8,128)(2,1)}, bf16[4096,512]{1,0:T(8,128)(2,1)}) custom-call(bf16[128,1536]{1,0:T(8,128)(2,1)} %bitcast.54, bf16[128,512]{1,0:T(8,128)(2,1)} %bitcast.59, bf16[128,2048]{1,0:T(8,128)(2,1)} %bitcast.52, bf16[512,512]{1,0:T(8,128)(2,1)} %bitcast.53), custom_call_target="tpu_custom_call" | custom-call | tf_op jit(solution)/shard_map/pallas_call | solution.py:345
  106.6 13.1 %shard_map.335 = (bf16[512,512]{1,0:T(8,128)(2,1)}, bf16[512,1536]{1,0:T(8,128)(2,1)}, f32[512,1024]{1,0:T(8,128)}, bf16[512,512]{1,0:T(8,128)(2,1)}, f32[512,512]{1,0:T(8,128)}) custom-call(bf16[2,196,512]{2,1,0:T(8,128)(2,1)} %copy.83.x_ref, bf16[256,196]{1,0:T(8,128)(2,1)} %constant.38.clone.place_ref, bf16[1024,1536]{1,0:T(8,128)(2,1)} %get-tuple-element.67.wqkv_ref, ...), custom_call_target="tpu_custom_call" | custom-call | flops 3221225472 | bytes 16777216 | tf_op jit(solution)/shard_map/pallas_call | solution.py:274
  119.7 8.4 %shard_map.336 = (bf16[2,196,512]{2,1,0:T(8,128)(2,1)}, bf16[512,512]{1,0:T(8,128)(2,1)}, bf16[512,2048]{1,0:T(8,128)(2,1)}, bf16[512,2048]{1,0:T(8,128)(2,1)}) custom-call(f32[512,512]{1,0:T(8,128)} %get-tuple-element.69.middle_ref, bf16[196,256]{1,0:T(8,128)(2,1)} %constant.40.clone.back_ref, bf16[1024,2048]{1,0:T(8,128)(2,1)} %get-tuple-element.70.wfc1_ref, ...), custom_call_target="tpu_custom_call" | custom-call | flops 3221225472 | bytes 16777216 | tf_op jit(solution)/shard_map/pallas_call | solution.py:274
  128.1 13.4 %shard_map.337 = (bf16[512,512]{1,0:T(8,128)(2,1)}, bf16[512,1536]{1,0:T(8,128)(2,1)}, f32[512,1024]{1,0:T(8,128)}, bf16[512,512]{1,0:T(8,128)(2,1)}, f32[512,512]{1,0:T(8,128)}) custom-call(bf16[2,196,512]{2,1,0:T(8,128)(2,1)} %get-tuple-element.72.x_ref, bf16[256,196]{1,0:T(8,128)(2,1)} %constant.39.clone.place_ref, ...), custom_call_target="tpu_custom_call" | custom-call | flops 3221225472 | bytes 16777216 | tf_op jit(solution)/shard_map/pallas_call | solution.py:274
  141.5 8.2 %shard_map.338 = (bf16[2,196,512]{2,1,0:T(8,128)(2,1)}, bf16[512,512]{1,0:T(8,128)(2,1)}, bf16[512,2048]{1,0:T(8,128)(2,1)}, bf16[512,2048]{1,0:T(8,128)(2,1)}) custom-call(f32[512,512]{1,0:T(8,128)} %get-tuple-element.73.middle_ref, bf16[196,256]{1,0:T(8,128)(2,1)} %constant.41.clone.back_ref, bf16[1024,2048]{1,0:T(8,128)(2,1)} %get-tuple-element.70.wfc1_ref, ...), custom_call_target="tpu_custom_call" | custom-call | flops 3221225472 | bytes 16777216 | tf_op jit(solution)/shard_map/pallas_call | solution.py:274
  149.7 11.2 %shard_map.339 = (bf16[512,2048]{1,0:T(8,128)(2,1)}, bf16[2048,512]{1,0:T(8,128)(2,1)}, f32[512,512]{1,0:T(8,128)}, f32[1,2048]{1,0:T(1,128)}, f32[1,512]{1,0:T(...) custom-call(bf16[2,196,512]{2,1,0:T(8,128)(2,1)} %copy.84.g_ref, bf16[256,196]{1,0:T(8,128)(2,1)} %constant.39.clone.place_ref, ...), custom_call_target="tpu_custom_call" | custom-call | flops 5368709120 | bytes 16777216 | tf_op jit(solution)/shard_map/pallas_call | solution.py:274
  160.9 17.1 %shard_map.340 = (bf16[512,1536]{1,0:T(8,128)(2,1)}, bf16[512,512]{1,0:T(8,128)(2,1)}, bf16[2,196,512]{2,1,0:T(8,128)(2,1)}, f32[1,1536]{1,0:T(1,128)}, f32[1,51...) custom-call(bf16[2,196,512]{2,1,0:T(8,128)(2,1)} %get-tuple-element.72.x_ref, ...), custom_call_target="tpu_custom_call" | custom-call | flops 8053063680 | bytes 16777216 | tf_op jit(solution)/shard_map/pallas_call | solution.py:274
  178.0 11.2 %shard_map.341 = (bf16[512,2048]{1,0:T(8,128)(2,1)}, bf16[2048,512]{1,0:T(8,128)(2,1)}, f32[512,512]{1,0:T(8,128)}, f32[1,2048]{1,0:T(1,128)}, f32[1,512]{1,0:T(...) custom-call(bf16[2,196,512]{2,1,0:T(8,128)(2,1)} %get-tuple-element.83.g_ref, bf16[256,196]{1,0:T(8,128)(2,1)} %constant.38.clone.place_ref, ...), custom_call_target="tpu_custom_call" | custom-call | flops 5368709120 | bytes 16777216 | tf_op jit(solution)/shard_map/pallas_call | solution.py:274
  189.3 16.9 %shard_map.342 = (bf16[512,1536]{1,0:T(8,128)(2,1)}, bf16[512,512]{1,0:T(8,128)(2,1)}, bf16[2,196,512]{2,1,0:T(8,128)(2,1)}, f32[1,1536]{1,0:T(1,128)}, f32[1,51...) custom-call(bf16[2,196,512]{2,1,0:T(8,128)(2,1)} %copy.83.x_ref, ...), custom_call_target="tpu_custom_call" | custom-call | flops 8053063680 | bytes 16777216 | tf_op jit(solution)/shard_map/pallas_call | solution.py:274
  206.3 0.7 reduce-scatter.29.cloned.1.call-update
  207.0 0.7 reduce-scatter.17.cloned.1.call-update
  209.2 1.4 fusion
  211.2 1.4 fusion.1
  214.5 26.6 %reduce-scatter.25.cloned.1.call-done = bf16[64,512]{1,0:T(8,128)(2,1)} async-done(((bf16[512,512]{1,0:T(8,128)(2,1)}), bf16[64,512]{1,0:T(8,128)(2,1)}) %reduce-scatter.25.cloned.1.call-update) | async-done | bytes 65552 | tf_op jit(solution)/shard_map/reduce_scatter | solution.py:457
  241.2 37.5 %reduce-scatter.29.cloned.1.call-done = bf16[64,512]{1,0:T(8,128)(2,1)} async-done(((bf16[512,512]{1,0:T(8,128)(2,1)}), bf16[64,512]{1,0:T(8,128)(2,1)}) %reduce-scatter.29.cloned.1.call-update) | async-done | bytes 65552 | tf_op jit(solution)/shard_map/reduce_scatter | solution.py:457
  278.8 41.7 %reduce-scatter.17.cloned.1.call-done = bf16[64,1536]{1,0:T(8,128)(2,1)} async-done(((bf16[512,1536]{1,0:T(8,128)(2,1)}), bf16[64,1536]{1,0:T(8,128)(2,1)}) %reduce-scatter.17.cloned.1.call-update) | async-done | bytes 196624 | tf_op jit(solution)/shard_map/reduce_scatter | solution.py:457
  320.6 41.5 %reduce-scatter.21.cloned.1.call-done = bf16[64,1536]{1,0:T(8,128)(2,1)} async-done(((bf16[512,1536]{1,0:T(8,128)(2,1)}), bf16[64,1536]{1,0:T(8,128)(2,1)}) %reduce-scatter.21.cloned.1.call-update) | async-done | bytes 196624 | tf_op jit(solution)/shard_map/reduce_scatter | solution.py:457
  362.8 0.7 reduce-scatter.45.cloned.1.call-update
  364.4 0.8 broadcast_select_fusion.14
  368.0 1.3 copy.77
  369.4 37.1 %reduce-scatter.37.cloned.1.call-done = bf16[64,2048]{1,0:T(8,128)(2,1)} async-done(((bf16[512,2048]{1,0:T(8,128)(2,1)}), bf16[64,2048]{1,0:T(8,128)(2,1)}) %reduce-scatter.37.cloned.1.call-update) | async-done | bytes 262160 | tf_op jit(solution)/shard_map/reduce_scatter | solution.py:457
  406.7 1.3 copy.78
  408.0 19.8 %reduce-scatter.27.cloned.1.call-done = bf16[16,512]{1,0:T(8,128)(2,1)} async-done(((bf16[64,512]{1,0:T(8,128)(2,1)}), bf16[16,512]{1,0:T(8,128)(2,1)}) %reduce-scatter.27.cloned.1.call-update) | async-done | bytes 16400 | tf_op jit(solution)/shard_map/reduce_scatter | solution.py:458
  427.7 13.3 %all_gather.30 = bf16[64,512]{1,0:T(8,128)(2,1)S(1)} all-gather(bf16[16,512]{1,0:T(8,128)(2,1)} %reduce-scatter.27.cloned.1.call-done), channel_id=1, replica_groups=mesh['section'=2,'fsdp'=4,'replica'=4] {'replica'}, dimensions={0}, use_global_device_ids=true | all-gather | bytes 81920 | tf_op jit(solution)/shard_map/all_gather | solution.py:459
  441.1 6.1 reduce-scatter.31.cloned.1.call-done
  447.1 13.5 %all_gather.31 = bf16[64,512]{1,0:T(8,128)(2,1)S(1)} all-gather(bf16[16,512]{1,0:T(8,128)(2,1)} %reduce-scatter.31.cloned.1.call-done), channel_id=1, replica_groups=mesh['section'=2,'fsdp'=4,'replica'=4] {'replica'}, dimensions={0}, use_global_device_ids=true | all-gather | bytes 81920 | tf_op jit(solution)/shard_map/all_gather | solution.py:459
  460.7 6.4 reduce-scatter.19.cloned.1.call-done
  467.1 14.2 %all_gather.28 = bf16[64,1536]{1,0:T(8,128)(2,1)S(1)} all-gather(bf16[16,1536]{1,0:T(8,128)(2,1)} %reduce-scatter.19.cloned.1.call-done), channel_id=1, replica_groups=mesh['section'=2,'fsdp'=4,'replica'=4] {'replica'}, dimensions={0}, use_global_device_ids=true | all-gather | bytes 245760 | tf_op jit(solution)/shard_map/all_gather | solution.py:459
  481.2 5.7 reduce-scatter.23.cloned.1.call-done
  486.9 13.8 %all_gather.29 = bf16[64,1536]{1,0:T(8,128)(2,1)S(1)} all-gather(bf16[16,1536]{1,0:T(8,128)(2,1)} %reduce-scatter.23.cloned.1.call-done), channel_id=1, replica_groups=mesh['section'=2,'fsdp'=4,'replica'=4] {'replica'}, dimensions={0}, use_global_device_ids=true | all-gather | bytes 245760 | tf_op jit(solution)/shard_map/all_gather | solution.py:459
  500.7 29.2 %reduce-scatter.33.cloned.1.call-done = bf16[64,2048]{1,0:T(8,128)(2,1)} async-done(((bf16[512,2048]{1,0:T(8,128)(2,1)}), bf16[64,2048]{1,0:T(8,128)(2,1)}) %reduce-scatter.33.cloned.1.call-update) | async-done | bytes 262160 | tf_op jit(solution)/shard_map/reduce_scatter | solution.py:457
  530.1 0.7 maximum_convert_fusion.3
  530.9 43.6 %reduce-scatter.45.cloned.1.call-done = bf16[256,512]{1,0:T(8,128)(2,1)} async-done(((bf16[2048,512]{1,0:T(8,128)(2,1)}), bf16[256,512]{1,0:T(8,128)(2,1)}) %reduce-scatter.45.cloned.1.call-update) | async-done | bytes 262160 | tf_op jit(solution)/shard_map/reduce_scatter | solution.py:457
  574.6 1.0 maximum_convert_fusion.2
  575.5 43.7 %reduce-scatter.41.cloned.1.call-done = bf16[256,512]{1,0:T(8,128)(2,1)} async-done(((bf16[2048,512]{1,0:T(8,128)(2,1)}), bf16[256,512]{1,0:T(8,128)(2,1)}) %reduce-scatter.41.cloned.1.call-update) | async-done | bytes 262160 | tf_op jit(solution)/shard_map/reduce_scatter | solution.py:457
  619.2 21.9 %reduce-scatter.39.cloned.1.call-done = bf16[16,2048]{1,0:T(8,128)(2,1)} async-done(((bf16[64,2048]{1,0:T(8,128)(2,1)}), bf16[16,2048]{1,0:T(8,128)(2,1)}) %reduce-scatter.39.cloned.1.call-update) | async-done | bytes 65552 | tf_op jit(solution)/shard_map/reduce_scatter | solution.py:458
  641.1 14.6 %all_gather.33 = bf16[64,2048]{1,0:T(8,128)(2,1)S(1)} all-gather(bf16[16,2048]{1,0:T(8,128)(2,1)} %reduce-scatter.39.cloned.1.call-done), channel_id=1, replica_groups=mesh['section'=2,'fsdp'=4,'replica'=4] {'replica'}, dimensions={0}, use_global_device_ids=true | all-gather | bytes 327680 | tf_op jit(solution)/shard_map/all_gather | solution.py:459
  655.7 5.4 reduce-scatter.35.cloned.1.call-done
  661.1 15.0 %all_gather.32 = bf16[64,2048]{1,0:T(8,128)(2,1)S(1)} all-gather(bf16[16,2048]{1,0:T(8,128)(2,1)} %reduce-scatter.35.cloned.1.call-done), channel_id=1, replica_groups=mesh['section'=2,'fsdp'=4,'replica'=4] {'replica'}, dimensions={0}, use_global_device_ids=true | all-gather | bytes 327680 | tf_op jit(solution)/shard_map/all_gather | solution.py:459
  676.2 5.2 reduce-scatter.47.cloned.1.call-done
  681.5 15.1 %all_gather.35 = bf16[256,512]{1,0:T(8,128)(2,1)S(1)} all-gather(bf16[64,512]{1,0:T(8,128)(2,1)} %reduce-scatter.47.cloned.1.call-done), channel_id=1, replica_groups=mesh['section'=2,'fsdp'=4,'replica'=4] {'replica'}, dimensions={0}, use_global_device_ids=true | all-gather | bytes 327680 | tf_op jit(solution)/shard_map/all_gather | solution.py:459
  696.6 5.4 reduce-scatter.43.cloned.1.call-done
  702.0 14.5 %all_gather.34 = bf16[256,512]{1,0:T(8,128)(2,1)S(1)} all-gather(bf16[64,512]{1,0:T(8,128)(2,1)} %reduce-scatter.43.cloned.1.call-done), channel_id=1, replica_groups=mesh['section'=2,'fsdp'=4,'replica'=4] {'replica'}, dimensions={0}, use_global_device_ids=true | all-gather | bytes 327680 | tf_op jit(solution)/shard_map/all_gather | solution.py:459
  716.7 1.1 maximum_convert_fusion
  718.2 1.1 maximum_convert_fusion.1
  (171 shorter events, 14.4 us)
Async XLA Ops:
  8.0 11.2 %copy-start = (s32[196]{0:T(256)S(1)}, s32[196]{0:T(256)}, u32[]{:S(2)}) copy-start(s32[196]{0:T(256)} %param.39) | copy-start | bytes 2356
  8.0 233.1 %reduce-scatter.25.cloned.1.call-start = ((), (), s32[]{:S(2)}) async-start(), calls=%async_computation.20 | async-start | bytes 589824 | tf_op jit(solution)/shard_map/reduce_scatter | solution.py:457
  22.0 0.6 copy-start.12
  24.9 1.2 copy-start.8
  25.0 1.4 copy-start.9
  206.2 2.4 copy-start.28
  206.2 2.4 copy-start.6
  206.2 72.5 %reduce-scatter.29.cloned.1.call-start = ((), (), s32[]{:S(2)}) async-start(), calls=%async_computation.22 | async-start | bytes 589824 | tf_op jit(solution)/shard_map/reduce_scatter | solution.py:457
  207.0 113.5 %reduce-scatter.17.cloned.1.call-start = ((), (), s32[]{:S(2)}) async-start(), calls=%async_computation.16 | async-start | bytes 1769472 | tf_op jit(solution)/shard_map/reduce_scatter | solution.py:457
  207.7 154.4 %reduce-scatter.21.cloned.1.call-start = ((), (), s32[]{:S(2)}) async-start(), calls=%async_computation.18 | async-start | bytes 1769472 | tf_op jit(solution)/shard_map/reduce_scatter | solution.py:457
  207.8 1.4 copy-start.13
  208.3 2.3 copy-start.7
  208.3 156.1 %all-reduce.4.cloned.1.call-start = ((), (), s32[]{:S(2)}) async-start(), calls=%async_computation.32 | async-start | bytes 151552 | tf_op jit(solution)/shard_map/psum | solution.py:452
  210.6 2.1 copy-start.25
  210.6 2.1 copy-start.16
  210.6 2.1 copy-start.29
  210.6 2.3 copy-start.24
  210.6 2.3 copy-start.20
  210.6 2.3 copy-start.19
  210.6 2.3 copy-start.14
  210.6 2.4 copy-start.18
  210.7 2.4 copy-start.27
  210.7 2.4 copy-start.17
  210.7 2.4 copy-start.26
  210.7 2.4 copy-start.23
  210.7 2.4 copy-start.22
  210.7 2.4 copy-start.15
  210.7 2.4 copy-start.21
  213.2 0.6 copy-start.11
  213.2 0.6 copy-start.10
  213.9 192.6 %reduce-scatter.37.cloned.1.call-start = ((), (), s32[]{:S(2)}) async-start(), calls=%async_computation.26 | async-start | bytes 2359296 | tf_op jit(solution)/shard_map/reduce_scatter | solution.py:457
  214.4 213.3 %reduce-scatter.27.cloned.1.call-start = ((), (), s32[]{:S(2)}) async-start(), calls=%async_computation.21 | async-start | bytes 81920 | tf_op jit(solution)/shard_map/reduce_scatter | solution.py:458
  241.1 206.0 %reduce-scatter.31.cloned.1.call-start = ((), (), s32[]{:S(2)}) async-start(), calls=%async_computation.23 | async-start | bytes 81920 | tf_op jit(solution)/shard_map/reduce_scatter | solution.py:458
  278.7 188.3 %reduce-scatter.19.cloned.1.call-start = ((), (), s32[]{:S(2)}) async-start(), calls=%async_computation.17 | async-start | bytes 245760 | tf_op jit(solution)/shard_map/reduce_scatter | solution.py:458
  320.5 166.4 %reduce-scatter.23.cloned.1.call-start = ((), (), s32[]{:S(2)}) async-start(), calls=%async_computation.19 | async-start | bytes 245760 | tf_op jit(solution)/shard_map/reduce_scatter | solution.py:458
  362.2 167.8 %reduce-scatter.33.cloned.1.call-start = ((), (), s32[]{:S(2)}) async-start(), calls=%async_computation.24 | async-start | bytes 2359296 | tf_op jit(solution)/shard_map/reduce_scatter | solution.py:457
  362.2 1.4 copy-start.2
  362.2 1.4 copy-start.3
  362.7 1.1 copy-start.4
  362.8 1.2 copy-start.5
  362.8 211.7 %reduce-scatter.45.cloned.1.call-start = ((), (), s32[]{:S(2)}) async-start(), calls=%async_computation.30 | async-start | bytes 2359296 | tf_op jit(solution)/shard_map/reduce_scatter | solution.py:457
  363.5 255.7 %reduce-scatter.41.cloned.1.call-start = ((), (), s32[]{:S(2)}) async-start(), calls=%async_computation.28 | async-start | bytes 2359296 | tf_op jit(solution)/shard_map/reduce_scatter | solution.py:457
  363.6 4.2 collective-permute-start
  364.0 5.3 collective-permute-start.1
  364.3 276.7 %reduce-scatter.39.cloned.1.call-start = ((), (), s32[]{:S(2)}) async-start(), calls=%async_computation.27 | async-start | bytes 327680 | tf_op jit(solution)/shard_map/reduce_scatter | solution.py:458
  406.5 254.6 %reduce-scatter.35.cloned.1.call-start = ((), (), s32[]{:S(2)}) async-start(), calls=%async_computation.25 | async-start | bytes 327680 | tf_op jit(solution)/shard_map/reduce_scatter | solution.py:458
  460.6 69.5 %collective-permute-start.3 = (bf16[64,512]{1,0:T(8,128)(2,1)S(1)}, bf16[64,512]{1,0:T(8,128)(2,1)S(1)}, u32[]{:S(2)}, u32[]{:S(2)}) collective-permute-start(bf16[64,512]{1,0:T(8,128)(2,1)S(1)} %broadcast_select_fusion.15), channel_id=1, source_target_pairs={{0,16},{16,0},{1,17},{17,1},{2,18},{18,2},{3,19},{19,3},{4,20},{20... | collective-permute-start | bytes 196616 | tf_op jit(solution)/shard_map/ppermute | solution.py:462
  529.9 151.5 %reduce-scatter.47.cloned.1.call-start = ((), (), s32[]{:S(2)}) async-start(), calls=%async_computation.31 | async-start | bytes 327680 | tf_op jit(solution)/shard_map/reduce_scatter | solution.py:458
  530.0 44.5 %collective-permute-start.2 = (bf16[64,1536]{1,0:T(8,128)(2,1)S(1)}, bf16[64,1536]{1,0:T(8,128)(2,1)S(1)}, u32[]{:S(2)}, u32[]{:S(2)}) collective-permute-start(bf16[64,1536]{1,0:T(8,128)(2,1)S(1)} %broadcast_select_fusion.12), channel_id=1, source_target_pairs={{0,16},{16,0},{1,17},{17,1},{2,18},{18,2},{3,19},{19,3},{4,20},{20... | collective-permute-start | bytes 589832 | tf_op jit(solution)/shard_map/ppermute | solution.py:462
  574.5 127.6 %reduce-scatter.43.cloned.1.call-start = ((), (), s32[]{:S(2)}) async-start(), calls=%async_computation.29 | async-start | bytes 327680 | tf_op jit(solution)/shard_map/reduce_scatter | solution.py:458
  676.2 40.5 %collective-permute-start.4 = (bf16[64,2048]{1,0:T(8,128)(2,1)S(1)}, bf16[64,2048]{1,0:T(8,128)(2,1)S(1)}, u32[]{:S(2)}, u32[]{:S(2)}) collective-permute-start(bf16[64,2048]{1,0:T(8,128)(2,1)S(1)} %broadcast_select_fusion.10), channel_id=1, source_target_pairs={{0,16},{16,0},{1,17},{17,1},{2,18},{18,2},{3,19},{19,3},{4,20},{20... | collective-permute-start | bytes 786440 | tf_op jit(solution)/shard_map/ppermute | solution.py:462
  716.6 1.6 collective-permute-start.5
  716.7 2.6 copy-start.1
Sparse Core Ops, SparseCore 0:
  206.4 34.6 reduce-scatter.24
  244.5 34.1 reduce-scatter.28
  282.0 38.4 reduce-scatter.16
  323.7 38.4 reduce-scatter.20
  365.3 41.1 reduce-scatter.36
  408.7 18.9 reduce-scatter.26
  429.9 17.1 reduce-scatter.30
  449.5 17.5 reduce-scatter.18
  469.3 17.5 reduce-scatter.22
  490.4 39.4 reduce-scatter.32
  533.2 41.1 reduce-scatter.44
  577.9 41.2 reduce-scatter.40
  621.4 19.6 reduce-scatter.38
  643.3 17.7 reduce-scatter.34
  663.2 18.1 reduce-scatter.46
  683.7 18.2 reduce-scatter.42
Sparse Core Ops, SparseCore 1:
  215.0 120.1 all-reduce.3
